TPU v7x, 32 devices: a whole 2x2x4 slice. The times are simulated.
32 devices in a mesh: cand: 4 (over x, core), row: 4 (over z), col: 2 (over y).
Axes of the slice: x: 2, y: 2, z: 4, core: 2. Of those that a mesh axis runs over, the one named last changes fastest.
Arguments:
- embedding: bfloat16 [1024, 1536], P(('row', 'col')), may hold values from -6 to 6
- bases_table: bfloat16 [4, 1536], replicated, may hold values from -10 to 10
- edit_pos: int32 [256], P('cand'), parts along dimension 0, may hold values from 0 to 1023
- edit_tok: int32 [256], P('cand'), parts along dimension 0, may hold values from 0 to 3
- w_row: bfloat16 [1536, 128], replicated, may hold values from -0.15625 to 0.15625
- w_col: bfloat16 [1536, 128], replicated, may hold values from -0.15625 to 0.15625
- dist_gain: float32 [128], replicated, may hold values from -4 to 4
- first_kernel: bfloat16 [3, 3, 128, 128], replicated, may hold values from -0.1875 to 0.1875
- second_kernel: bfloat16 [3, 3, 128, 128], replicated, may hold values from -0.1875 to 0.1875
- head_weight: bfloat16 [128], replicated, may hold values from -0.5 to 0.5
Outputs:
- contact: float32 [1024, 256], P(('cand', 'row'), 'col'), parts along dimension 0
There are 4 independent parts, one for each index of `cand`. A program takes and returns all parts, laid end to end along the dimension named above; an argument that names none is the same for every part. Nothing has to cross between parts.
Inputs may be any that keep to these rules, and one draw needn't show every extreme that they name: `edit_pos`: two substitutions may fall on the same input bin.
All inputs are finite; a program needn't handle non-finite values.
Results may differ from a plain program's by a relative error of at most 0.015.
Values may be sent and summed in bfloat16 or wider, within the bound.
No kernel may reach another device: no remote copies, remote signals or barrier semaphores. Data moves between devices by JAX's collectives and lax.ppermute only.
A program may use at most 64 MiB of HBM per device.

v0:
```python
import math

import jax
import jax.numpy as jnp
from jax import lax
from jax.sharding import PartitionSpec as P

POOL = 4
FIRST_SPACING = 2
SECOND_SPACING = 4
BASES = 4


def extended(cells, sides, width):
    for axis, dim in sides:
        count = lax.axis_size(axis)
        ends = count - 1
        head = lax.slice_in_dim(cells, 0, width, axis=dim)
        tail = lax.slice_in_dim(cells, cells.shape[dim] - width, cells.shape[dim], axis=dim)
        cells = jnp.concatenate(
            [
                lax.ppermute(tail, axis, [(i, (i + 1) % count) for i in range(ends)]),
                cells,
                lax.ppermute(head, axis, [((i + 1) % count, i) for i in range(ends)]),
            ],
            axis=dim,
        )
    return cells


def spaced_convolve(padded, weight, dilation, height, breadth):
    channels = padded.shape[2]
    summed = jnp.zeros((height * breadth, weight.shape[3]), jnp.float32)
    for a in range(3):
        for b in range(3):
            window = padded[
                dilation * a : dilation * a + height, dilation * b : dilation * b + breadth
            ]
            summed = summed + jnp.dot(
                window.reshape(height * breadth, channels),
                weight[a, b],
                preferred_element_type=jnp.float32,
            )
    return summed.reshape(height, breadth, weight.shape[3])


def on_device(
    embedding,
    bases_table,
    edit_pos,
    edit_tok,
    w_row,
    w_col,
    dist_gain,
    first_kernel,
    second_kernel,
    head_weight,
):
    n_rows = lax.axis_size("row")
    n_cols = lax.axis_size("col")
    row_at = lax.axis_index("row")
    col_at = lax.axis_index("col")
    shard_bins = embedding.shape[0]
    channels = embedding.shape[1]
    map_bins = shard_bins * n_rows * n_cols // POOL
    tile_row_count = map_bins // n_rows
    tile_column_count = map_bins // n_cols
    first_bin = (row_at * n_cols + col_at) * shard_bins
    local_bins = first_bin + jnp.arange(shard_bins, dtype=jnp.int32)
    pos_hot = (local_bins[:, None] == edit_pos[None, :]).astype(jnp.float32)
    base_hot = (edit_tok[:, None] == jnp.arange(BASES, dtype=jnp.int32)[None, :]).astype(
        jnp.float32
    )
    edit_rows = jnp.dot(base_hot, bases_table.astype(jnp.float32), precision=lax.Precision.HIGHEST)
    edit_delta = jnp.dot(pos_hot, edit_rows, precision=lax.Precision.HIGHEST)
    edited = embedding.astype(jnp.float32) + edit_delta
    pooled = jnp.mean(edited.reshape(shard_bins // POOL, POOL, channels), axis=1).astype(
        jnp.bfloat16
    )
    row_start = row_at * tile_row_count
    col_start = col_at * tile_column_count
    margin_pair = 0
    pair_rows = tile_row_count + 2 * margin_pair
    pair_cols = tile_column_count + 2 * margin_pair
    all_pooled = lax.all_gather(pooled, ("row", "col"), axis=0, tiled=True)
    row_feats = lax.dynamic_slice_in_dim(all_pooled, row_start, pair_rows, 0)
    col_feats = lax.dynamic_slice_in_dim(all_pooled, col_start, pair_cols, 0)
    row_proj = jnp.dot(row_feats, w_row, preferred_element_type=jnp.float32).astype(jnp.bfloat16)
    col_proj = jnp.dot(col_feats, w_col, preferred_element_type=jnp.float32).astype(jnp.bfloat16)
    row_bins = row_start - margin_pair + jnp.arange(pair_rows, dtype=jnp.int32)
    col_bins = col_start - margin_pair + jnp.arange(pair_cols, dtype=jnp.int32)
    distance = jnp.abs(row_bins[:, None] - col_bins[None, :]).astype(jnp.float32)
    dist_feat = jnp.log1p(distance) * (1.0 / math.log(map_bins))
    pair_inside = ((row_bins >= 0) & (row_bins < map_bins))[:, None] & (
        (col_bins >= 0) & (col_bins < map_bins)
    )[None, :]
    pair_value = jax.nn.relu(
        row_proj.astype(jnp.float32)[:, None, :]
        + col_proj.astype(jnp.float32)[None, :, :]
        + dist_gain[None, None, :] * dist_feat[:, :, None]
    )
    pair_grid = jnp.where(pair_inside[:, :, None], pair_value, 0.0).astype(jnp.bfloat16)
    pair_padded_map = extended(pair_grid, (("row", 0), ("col", 1)), FIRST_SPACING)
    first_layer = spaced_convolve(
        pair_padded_map, first_kernel, FIRST_SPACING, tile_row_count, tile_column_count
    )
    first_hidden = (pair_grid.astype(jnp.float32) + jax.nn.relu(first_layer)).astype(jnp.bfloat16)
    hidden_padded_map = extended(first_hidden, (("row", 0), ("col", 1)), SECOND_SPACING)
    second_layer = spaced_convolve(
        hidden_padded_map, second_kernel, SECOND_SPACING, tile_row_count, tile_column_count
    )
    second_hidden = first_hidden.astype(jnp.float32) + jax.nn.relu(second_layer)
    score = jnp.dot(
        second_hidden.reshape(tile_row_count * tile_column_count, -1),
        head_weight.astype(jnp.float32),
        precision=lax.Precision.HIGHEST,
    ).reshape(tile_row_count, tile_column_count)
    col_strip = lax.all_gather(score, "row", axis=0, tiled=True)
    row_block = lax.all_to_all(col_strip, "col", split_axis=0, concat_axis=1, tiled=True)
    mirrored = lax.dynamic_slice_in_dim(row_block, row_start, tile_row_count, 1)
    return 0.5 * (score + mirrored.T)


def solution(mesh):
    placed = (P(("row", "col"), None), P(), P("cand"), P("cand"), P(), P(), P(), P(), P(), P())
    return jax.shard_map(
        on_device, mesh=mesh, in_specs=placed, out_specs=P(("cand", "row"), "col"), check_vma=False
    )
```

profile of v0, /device:TPU:0, one launch (start us, length us, event | category | flops | bytes accessed | tf_op | source)
XLA Modules:
  0.0 127.5 jit_solution(369257005096935694)
XLA Ops:
  0.1 1.1 fusion.60
  1.1 1.5 %convolution_add_fusion.14 = f32[128,1536]{1,0:T(8,128)S(1)} fusion(f32[64,1536]{1,0:T(8,128)S(1)} %fusion.60, bf16[128,1536]{1,0:T(8,128)(2,1)} %param.10, s32[64]{0:T(128)} %param.12, s32[128]{0:T(128)S(1)} %iota_add_fusion), kind=kOutput, calls=%fused_computation.28 | convolution fusion | flops 151396352 | bytes 1573632 | tf_op jit(solution)/shard_map/dot_general | solution.py:75
  2.9 0.5 reduce_sum.9
  3.4 33.8 %all_gather.6 = bf16[256,1536]{1,0:T(8,128)(2,1)S(1)} all-gather(bf16[32,1536]{1,0:T(8,128)(2,1)S(1)} %multiply_convert_fusion), channel_id=1, replica_groups=mesh['cand'=4,'row'=4,'col'=2] {'row','col'}, dimensions={0}, use_global_device_ids=true | all-gather | bytes 884736 | tf_op jit(solution)/shard_map/all_gather | solution.py:85
  37.8 2.8 %select_convert_fusion = bf16[64,128,128]{2,1,0:T(8,128)(2,1)S(1)} fusion(f32[64,128]{1,0:T(8,128)S(1)} %log-plus-one_multiply_fusion, f32[128]{0:T(128)S(1)} %copy-done.5, pred[64,128]{1,0:T(8,128)(4,1)S(1)} %broadcast_and_fusion, f32[128,128]{1,0:T(8,128)S(1)} %fusion.8, f32[64,128]{1,0:T(8,128)S(1)} %fusion.9), kind=kLoop, calls=%fused_computation.25 | loop fusion | flops 6291456 | bytes 2236928 | tf_op jit(solution)/shard_map/convert_element_type | solution.py:102
  40.7 1.3 %collective-permute-start = (bf16[2,128,128]{2,1,0:T(8,128)(2,1)S(1)}, bf16[2,128,128]{2,1,0:T(8,128)(2,1)S(1)}, u32[]{:S(2)}, u32[]{:S(2)}) collective-permute-start(bf16[2,128,128]{2,1,0:T(8,128)(2,1)S(1)} %get-tuple-element.31), channel_id=1, source_target_pairs={{0,2},{2,4},{4,6},{1,3},{3,5},{5,7},{8,10},{10,12},{12,14},{9,11},... | collective-permute-start | bytes 196616 | tf_op jit(solution)/shard_map/ppermute | solution.py:22
  42.0 1.3 %collective-permute-start.1 = (bf16[2,128,128]{2,1,0:T(8,128)(2,1)S(1)}, bf16[2,128,128]{2,1,0:T(8,128)(2,1)S(1)}, u32[]{:S(2)}, u32[]{:S(2)}) collective-permute-start(bf16[2,128,128]{2,1,0:T(8,128)(2,1)S(1)} %get-tuple-element.32), channel_id=1, source_target_pairs={{2,0},{4,2},{6,4},{3,1},{5,3},{7,5},{10,8},{12,10},{14,12},{11,9},... | collective-permute-start | bytes 196616 | tf_op jit(solution)/shard_map/ppermute | solution.py:24
  43.5 0.4 collective-permute-done
  43.9 4.3 %collective-permute-done.1 = bf16[2,128,128]{2,1,0:T(8,128)(2,1)S(1)} collective-permute-done((bf16[2,128,128]{2,1,0:T(8,128)(2,1)S(1)}, bf16[2,128,128]{2,1,0:T(8,128)(2,1)S(1)}, u32[]{:S(2)}, u32[]{:S(2)}) %collective-permute-start.1) | collective-permute-done | bytes 65568 | tf_op jit(solution)/shard_map/ppermute | solution.py:24
  48.2 3.7 %collective-permute-start.2 = (bf16[68,2,128]{2,1,0:T(2,128)(2,1)S(1)}, bf16[68,2,128]{2,1,0:T(2,128)(2,1)S(1)}, u32[]{:S(2)}, u32[]{:S(2)}) collective-permute-start(bf16[68,2,128]{2,1,0:T(2,128)(2,1)S(1)} %get-tuple-element.23), channel_id=1, source_target_pairs={{0,1},{2,3},{4,5},{6,7},{8,9},{10,11},{12,13},{14,15},{16,17},{18,... | collective-permute-start | bytes 104456 | tf_op jit(solution)/shard_map/ppermute | solution.py:22
  52.0 1.5 %collective-permute-start.3 = (bf16[68,2,128]{2,1,0:T(2,128)(2,1)S(1)}, bf16[68,2,128]{2,1,0:T(2,128)(2,1)S(1)}, u32[]{:S(2)}, u32[]{:S(2)}) collective-permute-start(bf16[68,2,128]{2,1,0:T(2,128)(2,1)S(1)} %get-tuple-element.24), channel_id=1, source_target_pairs={{1,0},{3,2},{5,4},{7,6},{9,8},{11,10},{13,12},{15,14},{17,16},{19,... | collective-permute-start | bytes 104456 | tf_op jit(solution)/shard_map/ppermute | solution.py:24
  53.7 0.7 fusion.33
  54.4 3.4 %collective-permute-done.3 = bf16[68,2,128]{2,1,0:T(2,128)(2,1)S(1)} collective-permute-done((bf16[68,2,128]{2,1,0:T(2,128)(2,1)S(1)}, bf16[68,2,128]{2,1,0:T(2,128)(2,1)S(1)}, u32[]{:S(2)}, u32[]{:S(2)}) %collective-permute-start.3) | collective-permute-done | bytes 34848 | tf_op jit(solution)/shard_map/ppermute | solution.py:24
  57.8 3.2 %maximum_maximum_fusion.1 = (bf16[68,130,128]{2,1,0:T(8,128)(2,1)S(1)}, bf16[68,130,128]{2,1,0:T(8,128)(2,1)S(1)}) fusion(bf16[2,128,128]{2,1,0:T(8,128)(2,1)S(1)} %collective-permute-done.1, bf16[64,128,128]{2,1,0:T(8,128)(2,1)S(1)} %select_convert_fusion, bf16[2,128,128]{2,1,0:T(8,128)(2,1)S(1)} %collective-permute-done, ...), kind=kLoop, calls=%fused_computation.29 | loop fusion | flops 18104320 | bytes 6823936 | tf_op jit(solution)/shard_map/concatenate | solution.py:20
  61.0 2.8 %fusion.68 = (bf16[64,128,128]{2,1,0:T(8,128)(2,1)S(1)}, bf16[64,128,128]{2,1,0:T(8,128)(2,1)S(1)}, bf16[64,128,128]{2,1,0:T(8,128)(2,1)S(1)}, bf16[64,128,128]{...) fusion(bf16[68,130,128]{2,1,0:T(8,128)(2,1)S(1)} %get-tuple-element.21, ...), kind=kLoop, calls=%fused_computation.116 | loop fusion | bytes 25165824 | tf_op jit(solution)/shard_map/slice | solution.py:36
  63.8 0.7 fusion.25
  64.5 0.7 convolution_add_fusion.13
  65.2 0.7 convolution_add_fusion.12
  65.9 0.7 convolution_add_fusion.11
  66.6 0.7 convolution_add_fusion.10
  67.3 0.7 convolution_add_fusion.9
  68.0 0.7 convolution_add_fusion.8
  68.7 0.7 fusion.2
  69.4 2.5 %broadcast_add_fusion = (f32[64,128,128]{2,1,0:T(8,128)S(1)}, bf16[64,128,128]{2,1,0:T(8,128)(2,1)S(1)}) fusion(f32[128,128]{1,0:T(8,128)S(1)} %fusion.8, f32[64,128]{1,0:T(8,128)S(1)} %fusion.9, f32[64,128,128]{2,1,0:T(8,128)S(1)} %bitcast.135, f32[64,128]{1,0:T(8,128)S(1)} %log-plus-one_multiply_fusion, f32[128]{0:T(128)S(1)} %copy-done.5, ...), kind=kLoop, calls=%fused_computation.35 | loop fusion | flops 9437184 | bytes 10625536 | tf_op jit(solution)/shard_map/add | solution.py:98
  72.0 4.7 %collective-permute-start.4 = (bf16[4,128,128]{2,1,0:T(8,128)(2,1)S(1)}, bf16[4,128,128]{2,1,0:T(8,128)(2,1)S(1)}, u32[]{:S(2)}, u32[]{:S(2)}) collective-permute-start(bf16[4,128,128]{2,1,0:T(8,128)(2,1)S(1)} %get-tuple-element.27), channel_id=1, source_target_pairs={{0,2},{2,4},{4,6},{1,3},{3,5},{5,7},{8,10},{10,12},{12,14},{9,11},... | collective-permute-start | bytes 393224 | tf_op jit(solution)/shard_map/ppermute | solution.py:22
  76.7 1.3 %collective-permute-start.5 = (bf16[4,128,128]{2,1,0:T(8,128)(2,1)S(1)}, bf16[4,128,128]{2,1,0:T(8,128)(2,1)S(1)}, u32[]{:S(2)}, u32[]{:S(2)}) collective-permute-start(bf16[4,128,128]{2,1,0:T(8,128)(2,1)S(1)} %get-tuple-element.28), channel_id=1, source_target_pairs={{2,0},{4,2},{6,4},{3,1},{5,3},{7,5},{10,8},{12,10},{14,12},{11,9},... | collective-permute-start | bytes 393224 | tf_op jit(solution)/shard_map/ppermute | solution.py:24
  78.0 3.1 %add_convert_fusion.1 = bf16[8192,128]{1,0:T(8,128)(2,1)S(1)} fusion(f32[8192,128]{1,0:T(8,128)S(1)} %fusion.2, f32[64,128,128]{2,1,0:T(8,128)S(1)} %get-tuple-element.33, f32[8192]{0:T(1024)S(1)} %fusion.39, f32[128]{0:T(128)S(1)} %copy-done.5, pred[8192]{0:T(1024)(128)(4,1)S(1)} %bitcast_and_fusion), kind=kLoop, calls=%fused_computation.24 | loop fusion | flops 8388608 | bytes 10527232 | tf_op jit(solution)/shard_map/convert_element_type | solution.py:107
  81.2 2.4 %collective-permute-done.5 = bf16[4,128,128]{2,1,0:T(8,128)(2,1)S(1)} collective-permute-done((bf16[4,128,128]{2,1,0:T(8,128)(2,1)S(1)}, bf16[4,128,128]{2,1,0:T(8,128)(2,1)S(1)}, u32[]{:S(2)}, u32[]{:S(2)}) %collective-permute-start.5) | collective-permute-done | bytes 131104 | tf_op jit(solution)/shard_map/ppermute | solution.py:24
  83.6 1.6 %collective-permute-start.6 = (bf16[72,4,128]{2,1,0:T(4,128)(2,1)S(1)}, bf16[72,4,128]{2,1,0:T(4,128)(2,1)S(1)}, u32[]{:S(2)}, u32[]{:S(2)}) collective-permute-start(bf16[72,4,128]{2,1,0:T(4,128)(2,1)S(1)} %get-tuple-element.19), channel_id=1, source_target_pairs={{0,1},{2,3},{4,5},{6,7},{8,9},{10,11},{12,13},{14,15},{16,17},{18,... | collective-permute-start | bytes 221192 | tf_op jit(solution)/shard_map/ppermute | solution.py:22
  85.3 1.5 %collective-permute-start.7 = (bf16[72,4,128]{2,1,0:T(4,128)(2,1)S(1)}, bf16[72,4,128]{2,1,0:T(4,128)(2,1)S(1)}, u32[]{:S(2)}, u32[]{:S(2)}) collective-permute-start(bf16[72,4,128]{2,1,0:T(4,128)(2,1)S(1)} %get-tuple-element.20), channel_id=1, source_target_pairs={{1,0},{3,2},{5,4},{7,6},{9,8},{11,10},{13,12},{15,14},{17,16},{19,... | collective-permute-start | bytes 221192 | tf_op jit(solution)/shard_map/ppermute | solution.py:24
  86.8 0.4 pad_maximum_fusion.2
  87.2 0.7 fusion.22
  87.9 3.6 %collective-permute-done.7 = bf16[72,4,128]{2,1,0:T(4,128)(2,1)S(1)} collective-permute-done((bf16[72,4,128]{2,1,0:T(4,128)(2,1)S(1)}, bf16[72,4,128]{2,1,0:T(4,128)(2,1)S(1)}, u32[]{:S(2)}, u32[]{:S(2)}) %collective-permute-start.7) | collective-permute-done | bytes 73760 | tf_op jit(solution)/shard_map/ppermute | solution.py:24
  91.5 3.8 %maximum_maximum_fusion = (bf16[72,132,128]{2,1,0:T(8,128)(2,1)S(1)}, bf16[72,132,128]{2,1,0:T(8,128)(2,1)S(1)}) fusion(bf16[4,128,128]{2,1,0:T(8,128)(2,1)S(1)} %collective-permute-done.5, bf16[64,128,128]{2,1,0:T(8,128)(2,1)S(1)} %get-tuple-element.34, bf16[4,128,128]{2,1,0:T(8,128)(2,1)S(1)} %collective-permute-done.4, ...), kind=kLoop, calls=%fused_computation.26 | loop fusion | flops 19464192 | bytes 7372800 | tf_op jit(solution)/shard_map/concatenate | solution.py:20
  95.3 1.6 %fusion.66 = (bf16[64,128,128]{2,1,0:T(8,128)(2,1)S(1)}, bf16[64,128,128]{2,1,0:T(8,128)(2,1)S(1)}, bf16[64,128,128]{2,1,0:T(8,128)(2,1)S(1)}) fusion(bf16[72,132,128]{2,1,0:T(8,128)(2,1)S(1)} %get-tuple-element.17), kind=kLoop, calls=%fused_computation.114 | loop fusion | bytes 12582912 | tf_op jit(solution)/shard_map/slice | solution.py:36
  96.9 1.7 %fusion.67 = (bf16[64,128,128]{2,1,0:T(8,128)(2,1)S(1)}, bf16[64,128,128]{2,1,0:T(8,128)(2,1)S(1)}, bf16[64,128,128]{2,1,0:T(8,128)(2,1)S(1)}) fusion(bf16[72,132,128]{2,1,0:T(8,128)(2,1)S(1)} %get-tuple-element.18), kind=kLoop, calls=%fused_computation.115 | loop fusion | bytes 12582912 | tf_op jit(solution)/shard_map/slice | solution.py:36
  98.7 0.7 fusion.14
  99.3 0.7 convolution_add_fusion.6
  100.0 0.7 convolution_add_fusion.5
  100.8 0.7 convolution_add_fusion.4
  101.5 0.7 convolution_add_fusion.3
  102.2 0.7 convolution_add_fusion.2
  102.9 0.7 convolution_add_fusion.1
  103.6 0.9 fusion.4
  104.5 2.0 %fusion.64 = f32[1,64,128]{2,0,1:T(1,128)S(1)} fusion(f32[64,128,128]{2,1,0:T(8,128)S(1)} %bitcast.146, bf16[128]{0:T(256)(128)(2,1)S(1)} %copy-done.6), kind=kOutput, calls=%fused_computation.109 | convolution fusion | flops 12582912 | bytes 4227328 | tf_op jit(solution)/shard_map/dot_general | solution.py:113
  106.6 13.3 %all_gather.7 = f32[256,128]{1,0:T(8,128)S(1)} all-gather(f32[64,128]{1,0:T(8,128)S(1)} %bitcast.154), channel_id=1, replica_groups=mesh['cand'=4,'row'=4,'col'=2] {'row'}, dimensions={0}, use_global_device_ids=true | all-gather | bytes 163840 | tf_op jit(solution)/shard_map/all_gather | solution.py:118
  120.0 6.8 %all_to_all.19 = f32[2,128,128]{1,2,0:T(8,128)S(1)} all-to-all(f32[2,128,128]{1,2,0:T(8,128)S(1)} %copy.12), channel_id=1, replica_groups=mesh['cand'=4,'row'=4,'col'=2] {'col'}, dimensions={0} | all-to-all | bytes 262144 | tf_op jit(solution)/shard_map/all_to_all | solution.py:119
  126.9 0.6 fusion.13
  (37 shorter events, 1.6 us)
Async XLA Ops:
  0.0 37.4 %copy-start = (bf16[1536,128]{1,0:T(8,128)(2,1)S(1)}, bf16[1536,128]{1,0:T(8,128)(2,1)}, u32[]{:S(2)}) copy-start(bf16[1536,128]{1,0:T(8,128)(2,1)} %param.15) | copy-start | bytes 1179652
  0.0 37.2 %copy-start.2 = (bf16[1536,128]{1,0:T(8,128)(2,1)S(1)}, bf16[1536,128]{1,0:T(8,128)(2,1)}, u32[]{:S(2)}) copy-start(bf16[1536,128]{1,0:T(8,128)(2,1)} %param.14) | copy-start | bytes 1179652
  0.0 37.8 %copy-start.5 = (f32[128]{0:T(128)S(1)}, f32[128]{0:T(128)}, u32[]{:S(2)}) copy-start(f32[128]{0:T(128)} %param.16) | copy-start | bytes 1540
  40.7 3.2 %collective-permute-start = (bf16[2,128,128]{2,1,0:T(8,128)(2,1)S(1)}, bf16[2,128,128]{2,1,0:T(8,128)(2,1)S(1)}, u32[]{:S(2)}, u32[]{:S(2)}) collective-permute-start(bf16[2,128,128]{2,1,0:T(8,128)(2,1)S(1)} %get-tuple-element.31), channel_id=1, source_target_pairs={{0,2},{2,4},{4,6},{1,3},{3,5},{5,7},{8,10},{10,12},{12,14},{9,11},... | collective-permute-start | bytes 196616 | tf_op jit(solution)/shard_map/ppermute | solution.py:22
  42.0 6.2 %collective-permute-start.1 = (bf16[2,128,128]{2,1,0:T(8,128)(2,1)S(1)}, bf16[2,128,128]{2,1,0:T(8,128)(2,1)S(1)}, u32[]{:S(2)}, u32[]{:S(2)}) collective-permute-start(bf16[2,128,128]{2,1,0:T(8,128)(2,1)S(1)} %get-tuple-element.32), channel_id=1, source_target_pairs={{2,0},{4,2},{6,4},{3,1},{5,3},{7,5},{10,8},{12,10},{14,12},{11,9},... | collective-permute-start | bytes 196616 | tf_op jit(solution)/shard_map/ppermute | solution.py:24
  43.5 10.2 %copy-start.3 = (bf16[3,3,128,128]{3,2,1,0:T(8,128)(2,1)S(1)}, bf16[3,3,128,128]{3,2,1,0:T(8,128)(2,1)}, u32[]{:S(2)}) copy-start(bf16[3,3,128,128]{3,2,1,0:T(8,128)(2,1)} %param.17) | copy-start | bytes 884740
  48.2 6.2 %collective-permute-start.2 = (bf16[68,2,128]{2,1,0:T(2,128)(2,1)S(1)}, bf16[68,2,128]{2,1,0:T(2,128)(2,1)S(1)}, u32[]{:S(2)}, u32[]{:S(2)}) collective-permute-start(bf16[68,2,128]{2,1,0:T(2,128)(2,1)S(1)} %get-tuple-element.23), channel_id=1, source_target_pairs={{0,1},{2,3},{4,5},{6,7},{8,9},{10,11},{12,13},{14,15},{16,17},{18,... | collective-permute-start | bytes 104456 | tf_op jit(solution)/shard_map/ppermute | solution.py:22
  52.0 5.8 %collective-permute-start.3 = (bf16[68,2,128]{2,1,0:T(2,128)(2,1)S(1)}, bf16[68,2,128]{2,1,0:T(2,128)(2,1)S(1)}, u32[]{:S(2)}, u32[]{:S(2)}) collective-permute-start(bf16[68,2,128]{2,1,0:T(2,128)(2,1)S(1)} %get-tuple-element.24), channel_id=1, source_target_pairs={{1,0},{3,2},{5,4},{7,6},{9,8},{11,10},{13,12},{15,14},{17,16},{19,... | collective-permute-start | bytes 104456 | tf_op jit(solution)/shard_map/ppermute | solution.py:24
  72.0 9.2 %collective-permute-start.4 = (bf16[4,128,128]{2,1,0:T(8,128)(2,1)S(1)}, bf16[4,128,128]{2,1,0:T(8,128)(2,1)S(1)}, u32[]{:S(2)}, u32[]{:S(2)}) collective-permute-start(bf16[4,128,128]{2,1,0:T(8,128)(2,1)S(1)} %get-tuple-element.27), channel_id=1, source_target_pairs={{0,2},{2,4},{4,6},{1,3},{3,5},{5,7},{8,10},{10,12},{12,14},{9,11},... | collective-permute-start | bytes 393224 | tf_op jit(solution)/shard_map/ppermute | solution.py:22
  76.7 6.9 %collective-permute-start.5 = (bf16[4,128,128]{2,1,0:T(8,128)(2,1)S(1)}, bf16[4,128,128]{2,1,0:T(8,128)(2,1)S(1)}, u32[]{:S(2)}, u32[]{:S(2)}) collective-permute-start(bf16[4,128,128]{2,1,0:T(8,128)(2,1)S(1)} %get-tuple-element.28), channel_id=1, source_target_pairs={{2,0},{4,2},{6,4},{3,1},{5,3},{7,5},{10,8},{12,10},{14,12},{11,9},... | collective-permute-start | bytes 393224 | tf_op jit(solution)/shard_map/ppermute | solution.py:24
  81.1 6.0 %copy-start.4 = (bf16[3,3,128,128]{3,2,1,0:T(8,128)(2,1)S(1)}, bf16[3,3,128,128]{3,2,1,0:T(8,128)(2,1)}, u32[]{:S(2)}) copy-start(bf16[3,3,128,128]{3,2,1,0:T(8,128)(2,1)} %param.18) | copy-start | bytes 884740
  83.6 4.2 %collective-permute-start.6 = (bf16[72,4,128]{2,1,0:T(4,128)(2,1)S(1)}, bf16[72,4,128]{2,1,0:T(4,128)(2,1)S(1)}, u32[]{:S(2)}, u32[]{:S(2)}) collective-permute-start(bf16[72,4,128]{2,1,0:T(4,128)(2,1)S(1)} %get-tuple-element.19), channel_id=1, source_target_pairs={{0,1},{2,3},{4,5},{6,7},{8,9},{10,11},{12,13},{14,15},{16,17},{18,... | collective-permute-start | bytes 221192 | tf_op jit(solution)/shard_map/ppermute | solution.py:22
  85.3 6.2 %collective-permute-start.7 = (bf16[72,4,128]{2,1,0:T(4,128)(2,1)S(1)}, bf16[72,4,128]{2,1,0:T(4,128)(2,1)S(1)}, u32[]{:S(2)}, u32[]{:S(2)}) collective-permute-start(bf16[72,4,128]{2,1,0:T(4,128)(2,1)S(1)} %get-tuple-element.20), channel_id=1, source_target_pairs={{1,0},{3,2},{5,4},{7,6},{9,8},{11,10},{13,12},{15,14},{17,16},{19,... | collective-permute-start | bytes 221192 | tf_op jit(solution)/shard_map/ppermute | solution.py:24
  103.6 0.9 copy-start.6
  103.6 23.9 %copy-start.1 = (bf16[1536,128]{1,0:T(8,128)(2,1)S(1)}, bf16[1536,128]{1,0:T(8,128)(2,1)}, u32[]{:S(2)}) copy-start(bf16[1536,128]{1,0:T(8,128)(2,1)} %param.15) | copy-start | bytes 1179652
where the time goes:
time: 128 us; the launch traced here: 127 us
  blocking collectives  54 us (42%)
  matrix products  17.8 us (14%)
  other arithmetic  17.7 us (14%)
  starting transfers between devices  17 us (13%)
  waiting for transfers between devices  14.1 us (11%)
  local copies, waits for them, and re-layouts  6.55 us (5%)
    all_gather x1, blocking collectives, on_device(): all_pooled = lax.all_gather(pooled, ('row', 'col'), axis=0, tiled=True)  33.8 us
    ppermute x4, waiting for transfers between devices, extended(): lax.ppermute(head, axis, [((i + 1) % count, i) for i in range(ends)])  13.7 us
    all_gather x1, blocking collectives, on_device(): col_strip = lax.all_gather(score, 'row', axis=0, tiled=True)  13.3 us
    dot_general x18, matrix products, spaced_convolve(): jnp.dot(window.reshape(height * breadth, channels), weight[a, b], preferr...  12.7 us
    ppermute x4, starting transfers between devices, extended(): lax.ppermute(tail, axis, [(i, (i + 1) % count) for i in range(ends)])  11.4 us
    concatenate x4, other arithmetic, extended(): jnp.concatenate([lax.ppermute(tail, axis, [(i, (i + 1) % count) for i in...  7.64 us
    all_to_all x1, blocking collectives, on_device(): lax.all_to_all(col_strip, 'col', split_axis=0, concat_axis=1, tiled=True)  6.85 us
    slice x3, local copies, waits for them, and re-layouts, spaced_convolve(): padded[dilation * a:dilation * a + height, dilation * b:dilation * b + br...  6.15 us
  transfers between devices with their start and end apart: 8, of which 5 were waited for; matrix products, arithmetic and copies ran while one was open for 4% of the time, Pallas kernels for 0%

commit v1 on v0

v1 whole, which is shorter than its diff:
```python
import math

import jax
import jax.numpy as jnp
from jax import lax
from jax.sharding import PartitionSpec as P

POOL = 4
FIRST_SPACING = 2
SECOND_SPACING = 4
BASES = 4
MARGIN = FIRST_SPACING + SECOND_SPACING


def projected(embedding, bases_table, edit_pos, edit_tok, w_row, w_col, first_bin):
    shard_bins = embedding.shape[0]
    pooled_bins = shard_bins // POOL
    bins = first_bin // POOL + jnp.arange(pooled_bins, dtype=jnp.int32)
    in_bin = bins[:, None] == (edit_pos // POOL)[None, :]
    is_base = edit_tok[:, None] == jnp.arange(BASES, dtype=jnp.int32)[None, :]
    counts = jnp.dot(
        in_bin.astype(jnp.bfloat16), is_base.astype(jnp.bfloat16), preferred_element_type=jnp.float32
    ).astype(jnp.bfloat16)
    take = (
        jnp.arange(shard_bins, dtype=jnp.int32)[None, :] // POOL
        == jnp.arange(pooled_bins, dtype=jnp.int32)[:, None]
    ).astype(jnp.bfloat16)
    summed = jnp.dot(take, embedding, preferred_element_type=jnp.float32) + jnp.dot(
        counts, bases_table, preferred_element_type=jnp.float32
    )
    pooled = (summed * (1.0 / POOL)).astype(jnp.bfloat16)
    both = jnp.concatenate([w_row, w_col], axis=1)
    return jnp.dot(pooled, both, preferred_element_type=jnp.float32).astype(jnp.bfloat16)


def gathered(block):
    count = lax.axis_size(("row", "col"))
    copies = jnp.broadcast_to(block[None], (count, *block.shape))
    got = lax.all_to_all(copies, ("row", "col"), 0, 0)
    return got.reshape(count * block.shape[0], block.shape[1])


def mirrored_tile(score):
    n_rows, n_cols = lax.axis_size("row"), lax.axis_size("col")
    row_at, col_at = lax.axis_index("row"), lax.axis_index("col")
    height, breadth = score.shape
    size = min(height, breadth)
    wide = breadth > height
    parts = max(height, breadth) // size
    pieces = jnp.stack(
        [
            (score[:, k * size : (k + 1) * size] if wide else score[k * size : (k + 1) * size]).T
            for k in range(parts)
        ]
    )
    own = (row_at if wide else col_at) % parts
    received = []
    for turn in range(parts):
        pairs = []
        for r in range(n_rows):
            for c in range(n_cols):
                if wide:
                    to = (parts * c + (turn + r) % parts, r // parts)
                else:
                    to = (c // parts, parts * r + (turn + c) % parts)
                pairs.append((r * n_cols + c, to[0] * n_cols + to[1]))
        piece = lax.dynamic_index_in_dim(pieces, (own + turn) % parts, 0, keepdims=False)
        received.append(lax.ppermute(piece, ("row", "col"), pairs))
    stacked = jnp.stack(received)
    placed = [
        lax.dynamic_index_in_dim(stacked, (own - sub) % parts, 0, keepdims=False) for sub in range(parts)
    ]
    return jnp.concatenate(placed, axis=1 if wide else 0)


def spaced_convolve(padded, weight, dilation):
    return lax.conv_general_dilated(
        padded[None],
        weight,
        (1, 1),
        "VALID",
        rhs_dilation=(dilation, dilation),
        dimension_numbers=("NHWC", "HWIO", "NHWC"),
        preferred_element_type=jnp.float32,
    )[0]


def on_device(
    embedding,
    bases_table,
    edit_pos,
    edit_tok,
    w_row,
    w_col,
    dist_gain,
    first_kernel,
    second_kernel,
    head_weight,
):
    n_rows, n_cols = lax.axis_size("row"), lax.axis_size("col")
    row_at, col_at = lax.axis_index("row"), lax.axis_index("col")
    shard_bins = embedding.shape[0]
    map_bins = shard_bins * n_rows * n_cols // POOL
    height, breadth = map_bins // n_rows, map_bins // n_cols
    first_bin = (row_at * n_cols + col_at) * shard_bins
    block = projected(embedding, bases_table, edit_pos, edit_tok, w_row, w_col, first_bin)
    every = jnp.pad(gathered(block), ((MARGIN, MARGIN), (0, 0)))
    channels = w_row.shape[1]
    row_start, col_start = row_at * height, col_at * breadth
    pair_rows, pair_cols = height + 2 * MARGIN, breadth + 2 * MARGIN
    row_proj = lax.dynamic_slice(every, (row_start, 0), (pair_rows, channels))
    col_proj = lax.dynamic_slice(every, (col_start, channels), (pair_cols, channels))
    row_bins = row_start - MARGIN + jnp.arange(pair_rows, dtype=jnp.int32)
    col_bins = col_start - MARGIN + jnp.arange(pair_cols, dtype=jnp.int32)
    distance = jnp.abs(row_bins[:, None] - col_bins[None, :]).astype(jnp.float32)
    dist_feat = jnp.log1p(distance) * (1.0 / math.log(map_bins))
    inside = ((row_bins >= 0) & (row_bins < map_bins))[:, None] & (
        (col_bins >= 0) & (col_bins < map_bins)
    )[None, :]
    pair_value = jax.nn.relu(
        row_proj.astype(jnp.float32)[:, None, :]
        + col_proj.astype(jnp.float32)[None, :, :]
        + dist_gain[None, None, :] * dist_feat[:, :, None]
    )
    pair = jnp.where(inside[:, :, None], pair_value, 0.0).astype(jnp.bfloat16)
    edge = FIRST_SPACING
    hidden = pair[edge:-edge, edge:-edge].astype(jnp.float32) + jax.nn.relu(
        spaced_convolve(pair, first_kernel, FIRST_SPACING)
    )
    hidden = jnp.where(inside[edge:-edge, edge:-edge, None], hidden, 0.0).astype(jnp.bfloat16)
    edge = SECOND_SPACING
    last = hidden[edge:-edge, edge:-edge].astype(jnp.float32) + jax.nn.relu(
        spaced_convolve(hidden, second_kernel, SECOND_SPACING)
    )
    score = jnp.sum(last * head_weight.astype(jnp.float32), axis=2)
    return 0.5 * (score + mirrored_tile(score))


def solution(mesh):
    placed = (P(("row", "col"), None), P(), P("cand"), P("cand"), P(), P(), P(), P(), P(), P())
    return jax.shard_map(
        on_device, mesh=mesh, in_specs=placed, out_specs=P(("cand", "row"), "col"), check_vma=False
    )
```

time: 128 us -> 55.3 us (0.43)
  the two profiles are of different devices: /device:TPU:0 before, /device:TPU:4 now
where the time goes in v1:
time: 55.3 us; the launch traced here: 55 us
  matrix products  14.9 us (27%)
  starting transfers between devices  12.7 us (23%)
  other arithmetic  11.5 us (21%)
  waiting for transfers between devices  8.3 us (15%)
  local copies, waits for them, and re-layouts  7.28 us (13%)
    conv_general_dilated x2, matrix products, spaced_convolve(): lax.conv_general_dilated(padded[None], weight, (1, 1), 'VALID', rhs_dilat...  12.3 us
    all_to_all x1, starting transfers between devices, gathered(): got = lax.all_to_all(copies, ('row', 'col'), 0, 0)  6.33 us
    ppermute x2, starting transfers between devices, mirrored_tile(): received.append(lax.ppermute(piece, ('row', 'col'), pairs))  6.33 us
    convert_element_type x1, other arithmetic, on_device(): pair = jnp.where(inside[:, :, None], pair_value, 0.0).astype(jnp.bfloat16)  4.8 us
    all_to_all x1, waiting for transfers between devices, gathered(): got = lax.all_to_all(copies, ('row', 'col'), 0, 0)  4.4 us
    ppermute x2, waiting for transfers between devices, mirrored_tile(): received.append(lax.ppermute(piece, ('row', 'col'), pairs))  3.9 us
    convert_element_type x1, other arithmetic, on_device(): jnp.where(inside[edge:-edge, edge:-edge, None], hidden, 0.0)  3.84 us
    conv_general_dilated x4, local copies, waits for them, and re-layouts, spaced_convolve(): lax.conv_general_dilated(padded[None], weight, (1, 1), 'VALID', rhs_dilat...  1.93 us
  transfers between devices with their start and end apart: 3, of which 3 were waited for; matrix products, arithmetic and copies ran while one was open for 2% of the time, Pallas kernels for 0%

profile of v1, /device:TPU:4, one launch (start us, length us, event | category | flops | bytes accessed | tf_op | source)
XLA Modules:
  0.0 55.0 jit_solution(1816584361275991569)
XLA Ops:
  0.0 0.0 copy-start
  0.0 0.7 %and_select_fusion = s32[64]{0:T(128)S(1)} fusion(s32[64]{0:T(128)} %param.12), kind=kLoop, calls=%fused_computation.75 | loop fusion | flops 960 | bytes 512 | tf_op jit(solution)/shard_map/jit(floor_divide)/jit(_where)/select_n | solution.py:19
  0.7 0.3 copy-done
  1.0 0.2 fusion.49
  1.2 0.9 %convolution_convert_fusion = bf16[32,4]{0,1:T(4,128)(2,1)S(1)} fusion(s32[64]{0:T(128)} %param.13, s32[64]{0:T(128)S(1)} %and_select_fusion, s32[32]{0:T(128)S(1)} %iota_add_fusion.1), kind=kOutput, calls=%fused_computation.36 | convolution fusion | flops 18816 | bytes 896 | tf_op jit(solution)/shard_map/dot_general | solution.py:21
  2.1 1.5 %fusion.32 = bf16[32,256]{1,0:T(8,128)(2,1)S(1)} fusion(f32[32,1536]{1,0:T(8,128)S(1)} %fusion.49, bf16[32,4]{0,1:T(4,128)(2,1)S(1)} %convolution_convert_fusion, bf16[4,1536]{1,0:T(4,128)(2,1)} %param.11, bf16[1536,128]{1,0:T(8,128)(2,1)} %param.15, bf16[1536,128]{1,0:T(8,128)(2,1)} %param.14), kind=kOutput, calls=%fused_computation.35 | convolution fusion | flops 27287552 | bytes 1011968 | tf_op jit(solution)/shard_map/dot_general | solution.py:33
  3.6 0.7 %broadcast_in_dim.20 = bf16[8,32,256]{2,1,0:T(8,128)(2,1)} broadcast(bf16[32,256]{1,0:T(8,128)(2,1)S(1)} %fusion.32), dimensions={1,2} | broadcast | bytes 147456 | tf_op jit(solution)/shard_map/broadcast_in_dim | solution.py:38
  4.3 6.3 %all-to-all-start = ((bf16[8,32,256]{2,1,0:T(8,128)(2,1)}), bf16[8,32,256]{2,1,0:T(8,128)(2,1)S(1)}, u32[]{:S(2)}, u32[]{:S(2)}) async-start(bf16[8,32,256]{2,1,0:T(8,128)(2,1)} %broadcast_in_dim.20), calls=%async_computation | async-start | bytes 262144 | tf_op jit(solution)/shard_map/all_to_all | solution.py:39
  10.7 0.1 log-plus-one_multiply_fusion
  10.8 0.1 slice.27
  10.9 0.1 broadcast_and_fusion
  11.0 0.1 slice.24
  11.1 0.7 %convert_element_type.62 = f32[128]{0:T(128)S(1)} convert(bf16[128]{0:T(256)(128)(2,1)} %param.19) | non-fusion elementwise | flops 128 | bytes 768 | tf_op jit(solution)/shard_map/convert_element_type | solution.py:135
  11.8 4.4 %all-to-all-done = bf16[8,32,256]{2,1,0:T(8,128)(2,1)S(1)} async-done(((bf16[8,32,256]{2,1,0:T(8,128)(2,1)}), bf16[8,32,256]{2,1,0:T(8,128)(2,1)S(1)}, u32[]{:S(2)}, u32[]{:S(2)}) %all-to-all-start) | async-done | bytes 131104 | tf_op jit(solution)/shard_map/all_to_all | solution.py:39
  16.3 4.8 %fusion.22 = bf16[76,1,140,128]{3,0,2,1:T(8,128)(2,1)S(1)} fusion(f32[76,140]{0,1:T(8,128)S(1)} %log-plus-one_multiply_fusion, f32[128]{0:T(128)} %param.16, f32[140,128]{1,0:T(8,128)S(1)} %fusion.38, f32[76,128]{1,0:T(8,128)S(1)} %fusion.47, pred[76,140]{0,1:T(8,128)(4,1)S(1)} %broadcast_and_fusion), kind=kLoop, calls=%fused_computation.28 | loop fusion | flops 8171520 | bytes 2888144 | tf_op jit(solution)/shard_map/convert_element_type | solution.py:125
  21.1 0.5 pad.5
  21.6 0.0 copy-start.2
  21.6 0.0 copy-start.5
  21.6 1.1 %copy.19 = bf16[76,1,8,18,128]{4,2,3,0,1:T(8,128)(2,1)S(1)} copy(bf16[76,1,8,18,128]{4,0,3,2,1:T(8,128)(2,1)S(1)} %bitcast.59) | data formatting | bytes 5603328 | tf_op jit(solution)/shard_map/conv_general_dilated | solution.py:77
  22.7 0.2 slice.29
  22.9 0.0 copy-done.2
  22.9 0.0 copy-done.5
  22.9 6.7 %select_maximum_fusion = f32[72,8,18,128]{3,1,2,0:T(8,128)S(1)} fusion(pred[8,18]{0,1:T(8,128)(4,1)S(1)} %copy-done.5, bf16[3,3,128,128]{3,2,1,0:T(8,128)(2,1)S(1)} %copy-done.2, bf16[76,1,7,4,128]{4,2,3,0,1:T(8,128)(2,1)S(1)} %slice.29, bf16[76,1,8,18,128]{4,2,3,0,1:T(8,128)(2,1)S(1)} %copy.19), kind=kOutput, calls=%fused_computation.5 | convolution fusion | flops 3070574592 | bytes 8949904 | tf_op jit(solution)/shard_map/conv_general_dilated | solution.py:77
  29.6 0.0 copy-start.1
  29.6 1.7 %copy.20 = f32[72,8,18,128]{3,0,2,1:T(8,128)S(1)} copy(f32[72,8,18,128]{3,1,2,0:T(8,128)S(1)} %select_maximum_fusion) | data formatting | bytes 10616832 | tf_op jit(solution)/shard_map/jit(relu)/max | solution.py:127
  31.3 0.0 copy-done.1
  31.3 3.8 %fusion.4 = bf16[72,136,128]{2,0,1:T(8,128)(2,1)S(1)} fusion(f32[72,1,144,128]{3,0,2,1:T(8,128)S(1)} %bitcast.57, f32[72,136]{0,1:T(8,128)S(1)} %slice.27, f32[128]{0:T(128)S(1)} %copy-done.1, f32[136,128]{1,0:T(8,128)S(1)} %slice.26, f32[72,128]{1,0:T(8,128)S(1)} %slice.25, pred[72,136]{0,1:T(8,128)(4,1)S(1)} %slice.24), kind=kLoop, calls=%fused_computation.9 | loop fusion | flops 12533760 | bytes 7676224 | tf_op jit(solution)/shard_map/convert_element_type | solution.py:130
  35.2 0.0 copy-start.3
  35.2 0.0 copy-start.4
  35.2 0.3 copy.22
  35.5 0.4 slice.32
  35.9 0.2 copy-done.3
  36.1 0.0 copy-done.4
  36.1 5.6 %select_maximum_fusion.1 = f32[64,8,17,128]{3,1,2,0:T(8,128)S(1)} fusion(pred[8,17]{0,1:T(8,128)(4,1)S(1)} %copy-done.4, bf16[3,3,128,128]{3,2,1,0:T(8,128)(2,1)S(1)} %copy-done.3, bf16[72,1,7,8,128]{4,2,3,0,1:T(8,128)(2,1)S(1)} %slice.32, bf16[72,1,8,17,128]{4,2,3,0,1:T(8,128)(2,1)S(1)} %copy.22), kind=kOutput, calls=%fused_computation.11 | convolution fusion | flops 2580201472 | bytes 8290440 | tf_op jit(solution)/shard_map/conv_general_dilated | solution.py:77
  41.8 0.9 %copy.23 = f32[64,8,17,128]{3,0,2,1:T(8,128)S(1)} copy(f32[64,8,17,128]{3,1,2,0:T(8,128)S(1)} %select_maximum_fusion.1) | data formatting | bytes 8912896 | tf_op jit(solution)/shard_map/jit(relu)/max | solution.py:132
  42.6 1.2 %fusion.7 = f32[64,128]{0,1:T(8,128)S(1)} fusion(f32[64,1,136,128]{3,0,2,1:T(8,128)S(1)} %bitcast.58, bf16[72,136,128]{2,0,1:T(8,128)(2,1)S(1)} %fusion.4, f32[128]{0:T(128)S(1)} %convert_element_type.62), kind=kLoop, calls=%fused_computation.15 | loop fusion | flops 4186112 | bytes 6324736 | tf_op jit(solution)/shard_map/reduce_sum | solution.py:135
  43.9 3.6 %collective-permute-start = (f32[64,64]{1,0:T(8,128)S(1)}, f32[64,64]{1,0:T(8,128)S(1)}, u32[]{:S(2)}, u32[]{:S(2)}) collective-permute-start(f32[64,64]{1,0:T(8,128)S(1)} %get-tuple-element.8), channel_id=1, source_target_pairs={{0,0},{1,4},{2,2},{3,6},{4,1},{5,5},{6,3},{7,7},{8,8},{9,12},{10,1... | collective-permute-start | bytes 49160 | tf_op jit(solution)/shard_map/ppermute | solution.py:68
  47.4 2.8 %collective-permute-start.1 = (f32[64,64]{1,0:T(8,128)S(1)}, f32[64,64]{1,0:T(8,128)S(1)}, u32[]{:S(2)}, u32[]{:S(2)}) collective-permute-start(f32[64,64]{1,0:T(8,128)S(1)} %get-tuple-element.7), channel_id=1, source_target_pairs={{0,2},{1,6},{2,0},{3,4},{4,3},{5,7},{6,1},{7,5},{8,10},{9,14},{10,... | collective-permute-start | bytes 49160 | tf_op jit(solution)/shard_map/ppermute | solution.py:68
  50.2 2.0 %collective-permute-done = f32[64,64]{1,0:T(8,128)S(1)} collective-permute-done((f32[64,64]{1,0:T(8,128)S(1)}, f32[64,64]{1,0:T(8,128)S(1)}, u32[]{:S(2)}, u32[]{:S(2)}) %collective-permute-start) | collective-permute-done | bytes 16416 | tf_op jit(solution)/shard_map/ppermute | solution.py:68
  52.2 1.9 %collective-permute-done.1 = f32[64,64]{1,0:T(8,128)S(1)} collective-permute-done((f32[64,64]{1,0:T(8,128)S(1)}, f32[64,64]{1,0:T(8,128)S(1)}, u32[]{:S(2)}, u32[]{:S(2)}) %collective-permute-start.1) | collective-permute-done | bytes 16416 | tf_op jit(solution)/shard_map/ppermute | solution.py:68
  54.1 0.1 copy.24
  54.2 0.1 copy.25
  54.3 0.7 %copy.26 = f32[64,128]{1,0:T(8,128)} copy(f32[64,128]{0,1:T(8,128)S(1)} %fusion.37) | data formatting | bytes 65536 | tf_op jit(solution)/shard_map/mul | solution.py:136
  (14 shorter events, 0.2 us)
Async XLA Ops:
  0.0 1.0 %copy-start = (bf16[128,1536]{1,0:T(8,128)(2,1)S(1)}, bf16[128,1536]{1,0:T(8,128)(2,1)}, u32[]{:S(2)}) copy-start(bf16[128,1536]{1,0:T(8,128)(2,1)} %param.10) | copy-start | bytes 1179652
  4.3 11.9 %all-to-all-start = ((bf16[8,32,256]{2,1,0:T(8,128)(2,1)}), bf16[8,32,256]{2,1,0:T(8,128)(2,1)S(1)}, u32[]{:S(2)}, u32[]{:S(2)}) async-start(bf16[8,32,256]{2,1,0:T(8,128)(2,1)} %broadcast_in_dim.20), calls=%async_computation | async-start | bytes 262144 | tf_op jit(solution)/shard_map/all_to_all | solution.py:39
  21.6 1.3 %copy-start.2 = (bf16[3,3,128,128]{3,2,1,0:T(8,128)(2,1)S(1)}, bf16[3,3,128,128]{3,2,1,0:T(8,128)(2,1)}, u32[]{:S(2)}) copy-start(bf16[3,3,128,128]{3,2,1,0:T(8,128)(2,1)} %param.17) | copy-start | bytes 884740
  21.6 1.3 %copy-start.5 = (pred[8,18]{0,1:T(8,128)(4,1)S(1)}, pred[8,18]{0,1:T(8,128)(4,1)}, u32[]{:S(2)}) copy-start(pred[8,18]{0,1:T(8,128)(4,1)} %constant.121) | copy-start | bytes 436
  29.6 1.7 %copy-start.1 = (f32[128]{0:T(128)S(1)}, f32[128]{0:T(128)}, u32[]{:S(2)}) copy-start(f32[128]{0:T(128)} %param.16) | copy-start | bytes 1540
  35.2 1.0 %copy-start.3 = (bf16[3,3,128,128]{3,2,1,0:T(8,128)(2,1)S(1)}, bf16[3,3,128,128]{3,2,1,0:T(8,128)(2,1)}, u32[]{:S(2)}) copy-start(bf16[3,3,128,128]{3,2,1,0:T(8,128)(2,1)} %param.18) | copy-start | bytes 884740
  35.2 1.0 %copy-start.4 = (pred[8,17]{0,1:T(8,128)(4,1)S(1)}, pred[8,17]{0,1:T(8,128)(4,1)}, u32[]{:S(2)}) copy-start(pred[8,17]{0,1:T(8,128)(4,1)} %constant.122) | copy-start | bytes 412
  43.9 8.3 %collective-permute-start = (f32[64,64]{1,0:T(8,128)S(1)}, f32[64,64]{1,0:T(8,128)S(1)}, u32[]{:S(2)}, u32[]{:S(2)}) collective-permute-start(f32[64,64]{1,0:T(8,128)S(1)} %get-tuple-element.8), channel_id=1, source_target_pairs={{0,0},{1,4},{2,2},{3,6},{4,1},{5,5},{6,3},{7,7},{8,8},{9,12},{10,1... | collective-permute-start | bytes 49160 | tf_op jit(solution)/shard_map/ppermute | solution.py:68
  47.4 6.7 %collective-permute-start.1 = (f32[64,64]{1,0:T(8,128)S(1)}, f32[64,64]{1,0:T(8,128)S(1)}, u32[]{:S(2)}, u32[]{:S(2)}) collective-permute-start(f32[64,64]{1,0:T(8,128)S(1)} %get-tuple-element.7), channel_id=1, source_target_pairs={{0,2},{1,6},{2,0},{3,4},{4,3},{5,7},{6,1},{7,5},{8,10},{9,14},{10,... | collective-permute-start | bytes 49160 | tf_op jit(solution)/shard_map/ppermute | solution.py:68
